TPU v7x, 32 devices: a whole 2x2x4 slice. The times are simulated.
32 devices in a mesh: img: 2 (over x), row: 4 (over y, core), col: 4 (over z).
Axes of the slice: x: 2, y: 2, z: 4, core: 2. Of those that a mesh axis runs over, the one named last changes fastest.
Arguments:
- grid_elements: bfloat16 [256, 128, 768], P(('img', 'row'), 'col'), parts along dimension 0, may hold values from -6 to 6
- summary_vectors: bfloat16 [16, 8, 768], P(('img', 'row'), 'col'), parts along dimension 0, may hold values from -6 to 6
- triple_projection: bfloat16 [768, 2304], P(None, 'row'), may hold values from -0.375 to 0.375
- final_projection: bfloat16 [768, 768], P(None, 'row'), may hold values from -0.21875 to 0.21875
- genuine_flags: int32 [256, 128], P(('img', 'row'), 'col'), parts along dimension 0, may hold values 0 or 1
Outputs:
- element_result: bfloat16 [256, 128, 768], P(('img', 'row'), 'col'), parts along dimension 0
- summary_result: bfloat16 [16, 8, 768], P(('img', 'row'), 'col'), parts along dimension 0
There are 2 independent parts, one for each index of `img`. A program takes and returns all parts, laid end to end along the dimension named above; an argument that names none is the same for every part. Nothing has to cross between parts.
All inputs are finite; a program needn't handle non-finite values. No bound on the sum of `genuine_flags` on one device may be relied on, other than what follows from the above.
Results may differ from a plain program's by a relative error of at most 0.0096.
Values may be sent and summed in bfloat16 or wider, within the bound.
No kernel may reach another device: no remote copies, remote signals or barrier semaphores. Data moves between devices by JAX's collectives and lax.ppermute only.
A program may use at most 64 MiB of HBM per device.

v0:
```python
import functools

import jax
import jax.numpy as jnp
from jax import lax
from jax.experimental import pallas as pl
from jax.experimental.pallas import tpu as pltpu
from jax.sharding import PartitionSpec as P

HEAD_DIM = 64
PATCH_SIDE = 16
RADIUS = 4
TILE = 2 * RADIUS
LANES = 128
GROUP = 256
INVALID = 100.0
HIDDEN = -1e30
LOG2_E = 1.4426950408889634
EVEN_ROW, EVEN_COL, ROW, STARTS = 4, 5, 6, 7
VMEM_BYTES = 26 * 1024 * 1024


def nt(a, b):
    return lax.dot_general(a, b, (((1,), (1,)), ((), ())), preferred_element_type=jnp.float32)


def nn(a, b):
    return lax.dot_general(a, b, (((1,), (0,)), ((), ())), preferred_element_type=jnp.float32)


def layer_normalise(lines):
    center = lines - jnp.mean(lines, axis=-1, keepdims=True)
    spread = jnp.mean(center * center, axis=-1, keepdims=True)
    return center * lax.rsqrt(spread + 1e-05)


def pair_swapped(even_block, odd_block, axis):
    count = lax.axis_size(axis)
    got = []
    for first, block in ((0, even_block), (1, odd_block)):
        pairs = [(i, i + 1) for i in range(first, count - 1, 2)]
        got.append(lax.ppermute(block, axis, pairs + [(b, a) for a, b in pairs]))
    return got


def swapped(block, axis, bit):
    count = lax.axis_size(axis)
    return lax.ppermute(block, axis, [(i, i ^ bit) for i in range(count)])


def after(block, *others):
    return lax.optimization_barrier((block, *others))[0]


def bits_of(count):
    bits, bit = [], count // 2
    while bit:
        bits.append(bit)
        bit //= 2
    return bits


def marked_lanes(lines, hidden):
    first = jnp.where(hidden, INVALID, lines[:, :, :LANES])
    return jnp.concatenate([first, lines[:, :, LANES:]], axis=2)


def edge_kernel(piece_rows, place_ref, flags_hbm, x_hbm, triple_hbm, mark_ref, even_ref, odd_ref, mine_ref, last_ref, *scratch):
    flags_ref, first_s, last_s, spread, sems = scratch
    rows, cols = flags_ref.shape
    own_start = pl.multiple_of(place_ref[STARTS], 16)
    last_start = triple_hbm.shape[0] - last_ref.shape[0]
    copies = [
        pltpu.make_async_copy(x_hbm.at[0:RADIUS], first_s, sems.at[0]),
        pltpu.make_async_copy(x_hbm.at[rows - RADIUS : rows], last_s, sems.at[1]),
        pltpu.make_async_copy(triple_hbm.at[pl.ds(own_start, piece_rows), :], mine_ref, sems.at[2]),
        pltpu.make_async_copy(triple_hbm.at[last_start:, :], last_ref, sems.at[3]),
    ]
    flags_copy = pltpu.make_async_copy(flags_hbm, flags_ref, sems.at[4])
    flags_copy.start()
    for copy in copies:
        copy.start()
    flags_copy.wait()
    row_at = lax.broadcasted_iota(jnp.int32, (cols, cols), 0)
    diagonal = row_at == lax.broadcasted_iota(jnp.int32, (cols, cols), 1)
    for r in range(rows):
        hidden = jnp.where(flags_ref[r : r + 1, :] > 0, 0.0, INVALID)
        spread[r * cols : (r + 1) * cols, :] = jnp.where(diagonal, hidden, 0.0).astype(jnp.bfloat16)
    marks = nn(spread[...], jnp.ones((cols, LANES), jnp.bfloat16)).reshape(rows, cols, LANES)
    mark_ref[...] = marks.astype(jnp.bfloat16)
    for copy in copies:
        copy.wait()
    first, last = [
        marked_lanes(ref[...].astype(jnp.float32), marks[at] > INVALID / 2)
        for ref, at in ((first_s, slice(0, RADIUS)), (last_s, slice(rows - RADIUS, rows)))
    ]
    even = place_ref[EVEN_ROW] > 0
    even_ref[...] = jnp.where(even, last, first).astype(jnp.bfloat16)
    odd_ref[...] = jnp.where(even, first, last).astype(jnp.bfloat16)


def strip_kernel(place_ref, x_ref, mark_ref, even_rows_ref, odd_rows_ref, carriers_ref, even_ref, odd_ref, carriers_s):
    per_row = carriers_ref.shape[1]
    carriers_s[...] = jnp.zeros_like(carriers_s)
    for i in range(carriers_ref.shape[0]):
        carriers_s[i * per_row : (i + 1) * per_row, :] = carriers_ref[i].astype(jnp.float32)
    for i in range(carriers_s.shape[0] // TILE):
        even_ref[odd_ref.shape[0] + i] = carriers_s[i * TILE : (i + 1) * TILE, :].astype(jnp.bfloat16)
    rows, cols, channels = x_ref.shape
    middle = rows // 2
    low = lax.broadcasted_iota(jnp.int32, (1, TILE, 1), 1) < RADIUS
    even_row, even_col = place_ref[EVEN_ROW] > 0, place_ref[EVEN_COL] > 0
    for lane in range(0, channels, LANES):
        lanes = slice(lane, lane + LANES)
        strips = []
        for columns, last in ((slice(0, TILE), False), (slice(cols - TILE, cols), True)):

            def own(part):
                lines = x_ref[part, columns, lanes].astype(jnp.float32)
                if lane == 0:
                    lines = jnp.where(mark_ref[part, columns, :].astype(jnp.float32) > INVALID / 2, INVALID, lines)
                return lines

            even_rows = even_rows_ref[:, columns, lanes].astype(jnp.float32)
            odd_rows = odd_rows_ref[:, columns, lanes].astype(jnp.float32)
            top, bottom = jnp.where(even_row, odd_rows, even_rows), jnp.where(even_row, even_rows, odd_rows)
            upper = jnp.concatenate([top, own(slice(0, middle))], axis=0)
            lower = jnp.concatenate([own(slice(middle, rows)), bottom], axis=0)
            if last:
                upper = jnp.roll(upper, RADIUS, axis=1)
            else:
                lower = jnp.roll(lower, RADIUS, axis=1)
            strips.append(jnp.where(low, upper, lower))
        first, last = strips
        even_ref[: odd_ref.shape[0], :, lanes] = jnp.where(even_col, last, first).astype(jnp.bfloat16)
        odd_ref[:, :, lanes] = jnp.where(even_col, first, last).astype(jnp.bfloat16)


def own_kernel(x_ref, xq_ref):
    rows, cols, _ = x_ref.shape
    step = 4

    def own(i, _):
        at = pl.multiple_of(i * step, step)
        y = layer_normalise(x_ref[pl.ds(at, step)].astype(jnp.float32))
        for c in range(cols // TILE):
            piece = y[:, c * TILE : (c + 1) * TILE, :].reshape(step * TILE, -1)
            to = pl.multiple_of(c * rows * TILE + at * TILE, step * TILE)
            xq_ref[pl.ds(to, step * TILE), :] = piece.astype(jnp.bfloat16)
        return 0

    lax.fori_loop(0, rows // step, own, 0)


def halo_kernel(place_ref, xq_ref, mark_ref, even_rows_ref, odd_rows_ref, even_cols_ref, odd_cols_ref, xkv_ref, hide_ref, *scratch):
    rows, cols, _ = mark_ref.shape
    wide_rows, wide_cols = rows + 2 * RADIUS, cols + 2 * RADIUS
    half = wide_rows // 2
    step = 2
    top_s, bottom_s, left_s, right_s, top_ref, bottom_ref, left_ref, right_ref, flag_s = scratch
    for even, odd, low, high, low_flags, high_flags, parity, size in (
        (even_rows_ref, odd_rows_ref, top_s, bottom_s, top_ref, bottom_ref, EVEN_ROW, 2),
        (even_cols_ref, odd_cols_ref, left_s, right_s, left_ref, right_ref, EVEN_COL, 5),
    ):
        flip = place_ref[parity] > 0
        for i in range(0, odd.shape[0], size):
            a, b = even[i : i + size].astype(jnp.float32), odd[i : i + size].astype(jnp.float32)
            for lines, out, flags in ((jnp.where(flip, b, a), low, low_flags), (jnp.where(flip, a, b), high, high_flags)):
                out[i : i + size] = layer_normalise(lines)
                flags[i : i + size] = lines[:, :, :LANES]

    def lines_of(ref):
        return ref.astype(jnp.float32)

    def merge(at, blocks, left, right, to_ref):
        low = lax.broadcasted_iota(jnp.int32, (1, TILE, 1), 1) < RADIUS
        before = left
        for c in range(len(blocks) + 1):
            after = jnp.roll(blocks[c], RADIUS, axis=1) if c < len(blocks) else right
            to = c * wide_rows * TILE + at * TILE
            to = pl.multiple_of(to, step * TILE) if not isinstance(to, int) else to
            lines = jnp.where(low, before, after).reshape(step * TILE, -1)
            to_ref[pl.ds(to, step * TILE), :] = lines.astype(jnp.bfloat16)
            before = after

    def sides(at, upper, left_ref, right_ref, lanes):
        if upper:
            at = at - half
            left, right = jnp.roll(lines_of(left_ref[pl.ds(at, step), :, lanes]), RADIUS, axis=1), lines_of(
                right_ref[pl.ds(at, step), :, lanes]
            )
        else:
            left, right = lines_of(left_ref[pl.ds(at, step), :, lanes]), jnp.roll(
                lines_of(right_ref[pl.ds(at, step), :, lanes]), RADIUS, axis=1
            )
        return left, right

    every, few = slice(None), slice(0, LANES)

    def hide_if(border, lines):
        return jnp.where(place_ref[border] > 0, INVALID, lines)

    def mark_sides(at, upper):
        left, right = sides(at, upper, left_ref, right_ref, few)
        return hide_if(2, left), hide_if(3, right)

    def band(at, ref, ref_s, first, upper):
        cut = [slice(c * TILE, (c + 1) * TILE) for c in range(cols // TILE)]
        merge(at, [ref_s[first : first + step, k, :] for k in cut], *sides(at, upper, left_s, right_s, every), xkv_ref)
        marks = hide_if(int(upper), ref[first : first + step])
        beside = [hide_if(int(upper), side) for side in mark_sides(at, upper)]
        merge(at, [marks[:, k, :] for k in cut], *beside, flag_s)

    for i in range(0, RADIUS, step):
        band(i, top_ref, top_s, i, False)
        band(RADIUS + rows + i, bottom_ref, bottom_s, i, True)

    def middle(i, upper):
        at = pl.multiple_of(i * step, step)
        own = at - RADIUS
        blocks = []
        for c in range(cols // TILE):
            first = pl.multiple_of(c * rows * TILE + own * TILE, step * TILE)
            blocks.append(xq_ref[pl.ds(first, step * TILE), :].astype(jnp.float32).reshape(step, TILE, -1))
        merge(at, blocks, *sides(at, upper, left_s, right_s, every), xkv_ref)
        marks = mark_ref[pl.ds(own, step)].astype(jnp.float32)
        marks = [marks[:, c * TILE : (c + 1) * TILE, :] for c in range(cols // TILE)]
        merge(at, marks, *mark_sides(at, upper), flag_s)
        return 0

    lax.fori_loop(RADIUS // step, half // step, lambda i, _: middle(i, False), 0)
    lax.fori_loop(half // step, (RADIUS + rows) // step, lambda i, _: middle(i, True), 0)

    first_lane = (lax.broadcasted_iota(jnp.int32, (8, LANES), 1) == 0).astype(jnp.bfloat16)
    spans = []
    for c in range(wide_cols // TILE):
        lines = flag_s[c * wide_rows * TILE : (c + 1) * wide_rows * TILE, :]
        spans.append(jnp.where(nt(first_lane, lines) > INVALID / 2, HIDDEN, 0.0))
    tall = rows // TILE
    for c in range(cols // TILE):
        for r in range(tall):
            at = slice(r * TILE * TILE, r * TILE * TILE + 2 * TILE * TILE)
            hide_ref[c * tall + r] = jnp.concatenate([spans[c][:, at], spans[c + 1][:, at]], axis=1)


def project_kernel(whole, pieces, triple_rows, place_ref, *refs):
    sources, refs = refs[: len(whole) + len(pieces)], refs[len(whole) + len(pieces) :]
    xq_ref, xkv_ref, q_s, k_s, v_s, wt, sems = refs
    channels = wt.shape[1]
    groups = channels // GROUP
    factor = HEAD_DIM ** (-0.5) * LOG2_E
    me = place_ref[ROW]
    copies = []
    for j, source in enumerate(sources):
        if j < len(whole):
            to = (me ^ whole[j]) * triple_rows
        else:
            off, start = pieces[j - len(whole)]
            to = (me ^ off) * triple_rows + place_ref[STARTS + start]
        to = pl.multiple_of(to, 16)
        copy = pltpu.make_async_copy(source, wt.at[pl.ds(to, source.shape[0]), :], sems.at[j])
        copy.start()
        copies.append(copy)
    for copy in copies:
        copy.wait()

    q_rows, kv_rows = xq_ref.shape[0], xkv_ref.shape[0]
    q_chunk, kv_chunk = q_rows // 2, kv_rows // 4

    def project_q(n, _):
        w = wt[pl.ds(pl.multiple_of(n * GROUP, GROUP), GROUP), :]
        for m in range(0, q_rows, q_chunk):
            q_s[n, m : m + q_chunk, :] = (nt(xq_ref[m : m + q_chunk, :], w) * factor).astype(jnp.bfloat16)
        return 0

    def project_k(n, _):
        w = wt[pl.ds(pl.multiple_of(channels + n * GROUP, GROUP), GROUP), :]
        for m in range(0, kv_rows, kv_chunk):
            k_s[n, m : m + kv_chunk, :] = nt(xkv_ref[m : m + kv_chunk, :], w).astype(jnp.bfloat16)
        return 0

    def project_v(n, _):
        w = wt[pl.ds(pl.multiple_of(2 * channels + n * GROUP, GROUP), GROUP), :]
        for m in range(0, kv_rows, kv_chunk):
            y = nt(xkv_ref[m : m + kv_chunk, :], w).astype(jnp.bfloat16)
            for j in range(GROUP // LANES):
                v_s[GROUP // LANES * n + j, m : m + kv_chunk, :LANES] = y[:, j * LANES : (j + 1) * LANES]
                v_s[GROUP // LANES * n + j, m : m + kv_chunk, LANES:] = jnp.ones((kv_chunk, LANES), jnp.bfloat16)
        return 0

    lax.fori_loop(0, groups, project_q, 0)
    lax.fori_loop(0, groups, project_k, 0)
    lax.fori_loop(0, groups, project_v, 0)


def carrier_kernel(offsets, place_ref, wt, *refs):
    shards = len(offsets)
    finals, refs = refs[:shards], refs[shards:]
    summary_ref, wo, kce, vc_s, carriers_s, sems = refs
    per_row = summary_ref.shape[1]
    channels = wt.shape[1]
    groups = channels // GROUP
    heads = channels // HEAD_DIM
    factor = HEAD_DIM ** (-0.5)
    carriers_here = vc_s.shape[0]
    final_rows = wo.shape[0] // shards
    copies = []
    for j, off in enumerate(offsets):
        to = pl.multiple_of((place_ref[ROW] ^ off) * final_rows, 16)
        copy = pltpu.make_async_copy(finals[j].at[0:final_rows, :], wo.at[pl.ds(to, final_rows), :], sems.at[j])
        copy.start()
        copies.append(copy)
    coming = []
    sent = carriers_s.shape[0] // shards
    for j in range(shards):
        source = finals[j].at[final_rows : final_rows + sent, :]
        copy = pltpu.make_async_copy(source, carriers_s.at[j * sent : (j + 1) * sent, :], sems.at[shards + j])
        copy.start()
        coming.append(copy)
    for copy in coming:
        copy.wait()
    carriers = carriers_s[...].astype(jnp.float32)
    own = carriers[:carriers_here]
    carriers = layer_normalise(carriers).astype(jnp.bfloat16)
    own_norm = layer_normalise(own).astype(jnp.bfloat16)
    qc = (nt(own_norm, wt[:channels, :]) * factor).astype(jnp.bfloat16).astype(jnp.float32)
    kc = nt(carriers, wt[channels : 2 * channels, :]).astype(jnp.bfloat16)
    vc = nt(carriers, wt[2 * channels :, :]).astype(jnp.bfloat16)
    head_of = lax.broadcasted_iota(jnp.int32, (1, channels), 1) // HEAD_DIM
    stacked = jnp.concatenate([jnp.where(head_of == h, qc, 0.0) for h in range(heads)], axis=0)
    e = jnp.exp(nt(stacked.astype(jnp.bfloat16), kc))
    weights = (e / jnp.sum(e, axis=-1, keepdims=True)).astype(jnp.bfloat16)
    o = nn(weights, vc)
    mix = jnp.zeros((carriers_here, channels), jnp.float32)
    for h in range(heads):
        mix = jnp.where(head_of == h, o[h * carriers_here : (h + 1) * carriers_here, :], mix)
    for copy in copies:
        copy.wait()
    renewed = own + nt(mix.astype(jnp.bfloat16), wo[...])
    for i in range(summary_ref.shape[0]):
        summary_ref[i] = renewed[i * per_row : (i + 1) * per_row, :].astype(jnp.bfloat16)
    fresh = nt(layer_normalise(renewed).astype(jnp.bfloat16), wt[channels:, :]).astype(jnp.bfloat16).astype(jnp.float32)
    vc_s[...] = fresh[:, channels:]
    same = (
        lax.broadcasted_iota(jnp.int32, (GROUP, GROUP), 0) // HEAD_DIM
        == lax.broadcasted_iota(jnp.int32, (GROUP, GROUP), 1) // HEAD_DIM
    )
    windows = kce.shape[0] // groups
    for w in range(windows):
        for g in range(groups):
            kce[w * groups + g] = jnp.where(same, fresh[w : w + 1, g * GROUP : (g + 1) * GROUP], 0.0).astype(jnp.bfloat16)


def attend_kernel(x_ref, q_s, k_s, v_s, hide_ref, kce, vc_s, wo, out_hbm, out_ref, mix_s, out_sems):
    rows, cols, channels = x_ref.shape
    groups = channels // GROUP
    heads_in = GROUP // HEAD_DIM
    wide_rows = rows + 2 * RADIUS
    queries, span = TILE * TILE, 2 * TILE * TILE
    qi = lax.broadcasted_iota(jnp.int32, (queries, 2 * span), 0)
    ki = lax.broadcasted_iota(jnp.int32, (queries, 2 * span), 1)
    row_step = (ki % span) // TILE - qi // TILE
    col_step = (ki // span) * TILE + ki % TILE - qi % TILE
    seen = (row_step >= 0) & (row_step <= 2 * RADIUS) & (col_step >= 0) & (col_step <= 2 * RADIUS)
    band = jnp.where(seen, 0.0, HIDDEN)
    group_head = lax.broadcasted_iota(jnp.int32, (1, GROUP), 1) // HEAD_DIM
    only = [jnp.where(group_head == h, 1.0, 0.0).astype(jnp.bfloat16) for h in range(heads_in)]
    pair_head = lax.broadcasted_iota(jnp.int32, (1, LANES), 1) // HEAD_DIM
    pairs, in_pair = GROUP // LANES, LANES // HEAD_DIM
    tall, broad = rows // TILE, cols // TILE
    per_side = PATCH_SIDE // TILE

    def tile(t, _):
        c, r = t // tall, t % tall
        q_at = pl.multiple_of(c * (rows * TILE) + r * queries, queries)
        k0 = pl.multiple_of(c * (wide_rows * TILE) + r * queries, queries)
        k1 = pl.multiple_of(k0 + wide_rows * TILE, queries)
        window = (r // per_side) * (broad // per_side) + c // per_side
        bias = band + hide_ref[t][0:1, :]
        for g in range(groups):
            q = q_s[g, pl.ds(q_at, queries), :]
            qq = jnp.concatenate([q * mask for mask in only], axis=0)
            k = jnp.concatenate([k_s[g, pl.ds(k0, span), :], k_s[g, pl.ds(k1, span), :]], axis=0)
            p = jnp.exp2(nt(qq, k).reshape(heads_in, queries, 2 * span) + bias[None])
            p = p.reshape(heads_in * queries, 2 * span).astype(jnp.bfloat16)
            pc = jnp.exp2(nt(q, kce[window * groups + g]))
            v_new = vc_s[pl.ds(window, 1), g * GROUP : (g + 1) * GROUP]
            for j in range(pairs):
                v = jnp.concatenate(
                    [v_s[pairs * g + j, pl.ds(k0, span), :], v_s[pairs * g + j, pl.ds(k1, span), :]], axis=0
                )
                o = nn(p[j * in_pair * queries : (j + 1) * in_pair * queries, :], v)
                kept = o[:queries]
                for h in range(1, in_pair):
                    mine = o[h * queries : (h + 1) * queries]
                    kept = jnp.where(jnp.concatenate([pair_head] * 2, axis=1) == h, mine, kept)
                new = pc[:, j * LANES : (j + 1) * LANES]
                at = slice(g * GROUP + j * LANES, g * GROUP + (j + 1) * LANES)
                mixed = (kept[:, :LANES] + new * v_new[:, j * LANES : (j + 1) * LANES]) / (kept[:, LANES:] + new)
                mix_s[pl.ds(q_at, queries), at] = mixed.astype(jnp.bfloat16)
        return 0

    lax.fori_loop(0, tall * broad, tile, 0, unroll=2)

    going = []
    for pair in range(broad // 2):
        both = slice(2 * pair * TILE, 2 * (pair + 1) * TILE)
        for g in range(groups):
            at = slice(g * GROUP, (g + 1) * GROUP)
            w = wo[at, :]
            parts = [
                nt(mix_s[b * rows * TILE : (b + 1) * rows * TILE, :], w).reshape(rows, TILE, GROUP)
                for b in (2 * pair, 2 * pair + 1)
            ]
            y = jnp.concatenate(parts, axis=1) + x_ref[:, both, at].astype(jnp.float32)
            out_ref[pair, :, :, at] = y.astype(jnp.bfloat16)
        copy = pltpu.make_async_copy(out_ref.at[pair], out_hbm.at[:, both, :], out_sems.at[pair])
        copy.start()
        going.append(copy)
    for copy in going:
        copy.wait()


def local(grid_elements, summary_vectors, triple_projection, final_projection, genuine_flags):
    rows, cols, channels = grid_elements.shape
    wide_rows, wide_cols = rows + 2 * RADIUS, cols + 2 * RADIUS
    own = summary_vectors.reshape(-1, channels)

    triple_t, final_t = triple_projection.T, final_projection.T
    vmem = pl.BlockSpec(memory_space=pltpu.VMEM)
    anywhere = pl.BlockSpec(memory_space=pl.ANY)
    scalars = pl.BlockSpec(memory_space=pltpu.SMEM)
    hbm = pl.BlockSpec(memory_space=pltpu.HBM)
    small = pltpu.CompilerParams(vmem_limit_bytes=16 * 1024 * 1024)
    row_strip = jax.ShapeDtypeStruct((RADIUS, cols, channels), jnp.bfloat16)
    col_strip = jax.ShapeDtypeStruct((wide_rows // 2, 2 * RADIUS, channels), jnp.bfloat16)

    row, col, img = lax.axis_size("row"), lax.axis_size("col"), lax.axis_size("img")
    row_at, col_at, img_at = lax.axis_index("row"), lax.axis_index("col"), lax.axis_index("img")
    row_bits = bits_of(row)
    far, rest = row_bits[0], row_bits[1:]
    relays = img if triple_t.shape[0] % (16 * (img + 1)) == 0 else 0
    piece_rows = triple_t.shape[0] // (relays + 1)
    starts = [(img_at - k) % img for k in range(relays)] + [jnp.int32(relays)]
    place = [row_at == 0, row_at == row - 1, col_at == 0, col_at == col - 1, row_at % 2 == 0, col_at % 2 == 0, row_at]
    place = jnp.stack([jnp.asarray(p).astype(jnp.int32) for p in place + [start * piece_rows for start in starts]])

    mark, even_rows, odd_rows, mine, last = pl.pallas_call(
        functools.partial(edge_kernel, piece_rows),
        out_shape=(
            jax.ShapeDtypeStruct((rows, cols, LANES), jnp.bfloat16),
            row_strip,
            row_strip,
            jax.ShapeDtypeStruct((piece_rows, channels), jnp.bfloat16),
            jax.ShapeDtypeStruct((triple_t.shape[0] - relays * piece_rows, channels), jnp.bfloat16),
        ),
        in_specs=[scalars, hbm, hbm, hbm],
        out_specs=(vmem,) * 5,
        scratch_shapes=[
            pltpu.VMEM((rows, cols), jnp.int32),
            pltpu.VMEM(row_strip.shape, jnp.bfloat16),
            pltpu.VMEM(row_strip.shape, jnp.bfloat16),
            pltpu.VMEM((rows * cols, cols), jnp.bfloat16),
            pltpu.SemaphoreType.DMA((5,)),
        ],
        compiler_params=small,
        cost_estimate=pl.CostEstimate(flops=1_000_000, bytes_accessed=2_000_000, transcendentals=0),
        name="edge_rows",
    )(place, *(pltpu.with_memory_space_constraint(a, pltpu.HBM) for a in (genuine_flags, grid_elements, triple_t)))
    even_rows, odd_rows = pair_swapped(even_rows, odd_rows, "row")

    far_pieces = []
    if relays:
        first = swapped(mine, "row", far)
    far_last = swapped(after(last, even_rows, odd_rows), "row", far)

    carrier_tiles = -(-own.shape[0] // TILE)
    even_cols, odd_cols = pl.pallas_call(
        strip_kernel,
        out_shape=(jax.ShapeDtypeStruct((col_strip.shape[0] + carrier_tiles, *col_strip.shape[1:]), jnp.bfloat16), col_strip),
        in_specs=[scalars] + [vmem] * 5,
        out_specs=(vmem,) * 2,
        scratch_shapes=[pltpu.VMEM((carrier_tiles * TILE, channels), jnp.float32)],
        compiler_params=small,
        cost_estimate=pl.CostEstimate(flops=1_000_000, bytes_accessed=2_000_000, transcendentals=0),
        name="edge_columns",
    )(place, grid_elements, mark, even_rows, odd_rows, summary_vectors)
    even_cols, odd_cols = pair_swapped(even_cols, odd_cols, "col")
    carriers = even_cols[col_strip.shape[0] :].reshape(-1, channels)[: own.shape[0]]
    carriers = jnp.concatenate([own, carriers], axis=0)
    for bit in bits_of(col)[:-1]:
        got = swapped(carriers, "col", bit)
        carriers = jnp.concatenate([carriers, got], axis=0)
    if relays:
        first = after(first, even_cols, odd_cols)
        others = [lax.ppermute(first, "img", [(i, (i + k) % img) for i in range(img)]) for k in range(1, relays)]
        far_pieces = [first] + others
    far_pieces.append(far_last)

    final_pack = jnp.concatenate([final_t, carriers], axis=0)
    finals, triples, offsets = [final_pack], [triple_t], [0]
    for bit in rest:
        finals = finals + [swapped(p, "row", bit) for p in finals]
        triples = triples + [swapped(p, "row", bit) for p in triples]
        offsets = offsets + [o ^ bit for o in offsets]
    tiles = (rows // TILE) * (cols // TILE)
    keys = 4 * TILE * TILE
    xq = pl.pallas_call(
        own_kernel,
        out_shape=jax.ShapeDtypeStruct((rows * cols, channels), jnp.bfloat16),
        in_specs=[vmem],
        out_specs=vmem,
        compiler_params=small,
        cost_estimate=pl.CostEstimate(flops=10_000_000, bytes_accessed=3_000_000, transcendentals=1000),
        name="own_norm",
    )(grid_elements)
    xkv, hide = pl.pallas_call(
        halo_kernel,
        out_shape=(
            jax.ShapeDtypeStruct((wide_rows * wide_cols, channels), jnp.bfloat16),
            jax.ShapeDtypeStruct((tiles, 8, keys), jnp.float32),
        ),
        in_specs=[scalars] + [vmem] * 6,
        out_specs=(vmem,) * 2,
        scratch_shapes=[
            *[pltpu.VMEM(shape.shape, jnp.float32) for shape in (row_strip, row_strip, col_strip, col_strip)],
            *[pltpu.VMEM((*shape.shape[:2], LANES), jnp.float32) for shape in (row_strip, row_strip, col_strip, col_strip)],
            pltpu.VMEM((wide_rows * wide_cols, LANES), jnp.bfloat16),
        ],
        compiler_params=pltpu.CompilerParams(vmem_limit_bytes=24 * 1024 * 1024),
        cost_estimate=pl.CostEstimate(flops=10_000_000, bytes_accessed=6_000_000, transcendentals=1000),
        name="halo_norm",
    )(place, after(xq, got), mark, even_rows, odd_rows, even_cols, odd_cols)

    far_final = swapped(final_pack, "row", far)

    far_offsets = [far]
    far_pieces = [[after(piece, xkv)] for piece in far_pieces]
    for bit in rest:
        far_pieces = [same + [swapped(p, "row", bit) for p in same] for same in far_pieces]
        far_offsets = far_offsets + [o ^ bit for o in far_offsets]

    groups = channels // GROUP
    numbered = [(off, number) for number in range(len(far_pieces)) for off in far_offsets]
    sources = triples + [piece for same in far_pieces for piece in same]
    q, k, v, wt = pl.pallas_call(
        functools.partial(project_kernel, offsets, numbered, triple_t.shape[0]),
        out_shape=(
            jax.ShapeDtypeStruct((groups, rows * cols, GROUP), jnp.bfloat16),
            jax.ShapeDtypeStruct((groups, wide_rows * wide_cols, GROUP), jnp.bfloat16),
            jax.ShapeDtypeStruct((channels // LANES, wide_rows * wide_cols, 2 * LANES), jnp.bfloat16),
            jax.ShapeDtypeStruct((3 * channels, channels), jnp.bfloat16),
        ),
        in_specs=[scalars] + [anywhere] * len(sources) + [vmem] * 2,
        out_specs=(vmem,) * 4,
        scratch_shapes=[pltpu.SemaphoreType.DMA((len(sources),))],
        compiler_params=pltpu.CompilerParams(vmem_limit_bytes=VMEM_BYTES),
        cost_estimate=pl.CostEstimate(flops=5_000_000_000, bytes_accessed=14_000_000, transcendentals=0),
        name="project",
    )(place, *sources, xq, xkv)

    far_finals = [after(far_final, q)]
    for bit in rest:
        far_finals = far_finals + [swapped(p, "row", bit) for p in far_finals]
    finals, offsets = finals + far_finals, offsets + far_offsets
    carriers_here = carrier_tiles * TILE
    summary_result, wo, kce, vc = pl.pallas_call(
        functools.partial(carrier_kernel, offsets),
        out_shape=(
            jax.ShapeDtypeStruct(summary_vectors.shape, jnp.bfloat16),
            jax.ShapeDtypeStruct((channels, channels), jnp.bfloat16),
            jax.ShapeDtypeStruct((own.shape[0] * groups, GROUP, GROUP), jnp.bfloat16),
            jax.ShapeDtypeStruct((carriers_here, channels), jnp.float32),
        ),
        in_specs=[scalars, vmem] + [anywhere] * len(finals),
        out_specs=(vmem,) * 4,
        scratch_shapes=[
            pltpu.VMEM((row * col * own.shape[0], channels), jnp.bfloat16),
            pltpu.SemaphoreType.DMA((2 * len(finals),)),
        ],
        compiler_params=pltpu.CompilerParams(vmem_limit_bytes=VMEM_BYTES),
        cost_estimate=pl.CostEstimate(flops=500_000_000, bytes_accessed=5_000_000, transcendentals=10_000),
        name="carriers",
    )(place, wt, *finals)

    out = pl.pallas_call(
        attend_kernel,
        out_shape=jax.ShapeDtypeStruct(grid_elements.shape, jnp.bfloat16),
        in_specs=[vmem] * 8,
        out_specs=anywhere,
        scratch_shapes=[
            pltpu.VMEM((cols // (2 * TILE), rows, 2 * TILE, channels), jnp.bfloat16),
            pltpu.VMEM((rows * cols, channels), jnp.bfloat16),
            pltpu.SemaphoreType.DMA((cols // (2 * TILE),)),
        ],
        compiler_params=pltpu.CompilerParams(vmem_limit_bytes=VMEM_BYTES),
        cost_estimate=pl.CostEstimate(flops=5_000_000_000, bytes_accessed=12_000_000, transcendentals=4_000_000),
        name="attend",
    )(grid_elements, q, k, v, hide, kce, vc, wo)
    return (out, summary_result)


def solution(mesh):
    placed = (
        P(("img", "row"), "col", None),
        P(("img", "row"), "col", None),
        P(None, "row"),
        P(None, "row"),
        P(("img", "row"), "col"),
    )
    return jax.shard_map(
        local,
        mesh=mesh,
        in_specs=placed,
        out_specs=(P(("img", "row"), "col", None), P(("img", "row"), "col", None)),
        check_vma=False,
    )
```

profile of v0, /device:TPU:0, one launch (start us, length us, event | category | flops | bytes accessed | tf_op | source)
XLA Modules:
  0.0 64.2 jit_solution(9046005246342172465)
XLA Ops:
  0.6 0.0 copy-start
  0.7 0.1 stack.63.place_ref
  0.8 2.6 %edge_rows.1 = (bf16[32,32,128]{2,1,0:T(8,128)(2,1)S(1)}, bf16[4,32,768]{2,1,0:T(8,128)(2,1)S(1)}, bf16[4,32,768]{2,1,0:T(8,128)(2,1)S(1)}, bf16[192,768]{1,0:T(8,128)(2,1)}, bf16[192,768]{1,0:T(8,128)(2,1)S(1)}) custom-call(s32[10]{0:T(128)S(1)} %stack.63.place_ref, s32[32,32]{1,0:T(8,128)} %flags_hbm.1, bf16[32,32,768]{2,1,0:T(8,128)(2,1)} %x_ref.5, ...), custom_call_target="tpu_custom_call" | custom-call | flops 1000000 | bytes 2000000 | tf_op jit(solution)/shard_map/edge_rows/pallas_call | solution.py:448
  3.4 0.7 %copy-done.3 = bf16[192,768]{1,0:T(8,128)(2,1)} copy-done((bf16[192,768]{1,0:T(8,128)(2,1)}, bf16[192,768]{1,0:T(8,128)(2,1)S(1)}, u32[]{:S(2)}) %copy-start.3) | copy-done | bytes 294936
  4.1 0.5 collective-permute-start.2
  4.5 0.7 %collective-permute-start.3 = (bf16[4,32,768]{2,1,0:T(8,128)(2,1)S(1)}, bf16[4,32,768]{2,1,0:T(8,128)(2,1)S(1)}, u32[]{:S(2)}, u32[]{:S(2)}) collective-permute-start(bf16[4,32,768]{2,1,0:T(8,128)(2,1)S(1)} %get-tuple-element.29), channel_id=1, source_target_pairs={{4,8},{8,4},{5,9},{9,5},{6,10},{10,6},{7,11},{11,7},{20,24},{24,20... | collective-permute-start | bytes 589832 | tf_op jit(solution)/shard_map/ppermute | solution.py:42
  5.2 4.0 %collective-permute-start.1 = (bf16[192,768]{1,0:T(8,128)(2,1)}, bf16[192,768]{1,0:T(8,128)(2,1)}, u32[]{:S(2)}, u32[]{:S(2)}) collective-permute-start(bf16[192,768]{1,0:T(8,128)(2,1)} %get-tuple-element.26), channel_id=1, source_target_pairs={{0,8},{4,12},{8,0},{12,4},{1,9},{5,13},{9,1},{13,5},{2,10},{6,14},... | collective-permute-start | bytes 884744 | tf_op jit(solution)/shard_map/ppermute | solution.py:48
  9.2 0.0 collective-permute-done.2.even_rows_ref
  9.2 0.0 collective-permute-done.3.odd_rows_ref
  9.2 1.7 %edge_columns.1 = (bf16[21,8,768]{2,1,0:T(8,128)(2,1)}, bf16[20,8,768]{2,1,0:T(8,128)(2,1)}) custom-call(s32[10]{0:T(128)S(1)} %stack.63.place_ref, bf16[32,32,768]{2,1,0:T(8,128)(2,1)S(1)} %copy-done, bf16[32,32,128]{2,1,0:T(8,128)(2,1)S(1)} %get-tuple-element.27.mark_ref, bf16[4,32,768]{2,1,0:T(8,128)(2,1)S(1)} %collective-permute-done.2.even_rows_ref, ...), custom_call_target="tpu_custom_call" | custom-call | flops 1000000 | bytes 2000000 | tf_op jit(solution)/shard_map/edge_columns/pallas_call | solution.py:478
  10.9 2.1 %collective-permute-start.4 = (bf16[21,8,768]{2,1,0:T(8,128)(2,1)}, bf16[21,8,768]{2,1,0:T(8,128)(2,1)S(1)}, u32[]{:S(2)}, u32[]{:S(2)}) collective-permute-start(bf16[21,8,768]{2,1,0:T(8,128)(2,1)} %get-tuple-element.30), channel_id=1, source_target_pairs={{0,1},{2,3},{1,0},{3,2},{4,5},{6,7},{5,4},{7,6},{8,9},{10,11},{9,8... | collective-permute-start | bytes 774152 | tf_op jit(solution)/shard_map/ppermute | solution.py:42
  12.9 1.4 %collective-permute-start.5 = (bf16[20,8,768]{2,1,0:T(8,128)(2,1)}, bf16[20,8,768]{2,1,0:T(8,128)(2,1)}, u32[]{:S(2)}, u32[]{:S(2)}) collective-permute-start(bf16[20,8,768]{2,1,0:T(8,128)(2,1)} %get-tuple-element.31), channel_id=1, source_target_pairs={{1,2},{2,1},{5,6},{6,5},{9,10},{10,9},{13,14},{14,13},{17,18},{18,... | collective-permute-start | bytes 737288 | tf_op jit(solution)/shard_map/ppermute | solution.py:42
  14.3 4.2 %collective-permute-start = (bf16[576,768]{1,0:T(8,128)(2,1)S(1)}, bf16[576,768]{1,0:T(8,128)(2,1)}, u32[]{:S(2)}, u32[]{:S(2)}) collective-permute-start(bf16[576,768]{1,0:T(8,128)(2,1)S(1)} %bitcast.14), channel_id=1, source_target_pairs={{0,4},{4,0},{8,12},{12,8},{1,5},{5,1},{9,13},{13,9},{2,6},{6,2},{1... | collective-permute-start | bytes 2654216 | tf_op jit(solution)/shard_map/ppermute | solution.py:48
  18.5 1.1 %collective-permute-start.10 = (bf16[192,768]{1,0:T(8,128)(2,1)}, bf16[192,768]{1,0:T(8,128)(2,1)S(1)}, u32[]{:S(2)}, u32[]{:S(2)}) collective-permute-start(bf16[192,768]{1,0:T(8,128)(2,1)} %copy-done.3), channel_id=1, source_target_pairs={{0,8},{4,12},{8,0},{12,4},{1,9},{5,13},{9,1},{13,5},{2,10},{6,14},... | collective-permute-start | bytes 884744 | tf_op jit(solution)/shard_map/ppermute | solution.py:48
  19.6 0.0 collective-permute-done.4.even_cols_ref
  19.6 1.6 %collective-permute-start.8 = (bf16[192,768]{1,0:T(8,128)(2,1)}, bf16[192,768]{1,0:T(8,128)(2,1)S(1)}, u32[]{:S(2)}, u32[]{:S(2)}) collective-permute-start(bf16[192,768]{1,0:T(8,128)(2,1)} %collective-permute-done.1.refs_2_), channel_id=1, source_target_pairs={{0,16},{16,0},{1,17},{17,1},{2,18},{18,2},{3,19},{19,3},{4,20},{20... | collective-permute-start | bytes 884744 | tf_op jit(solution)/shard_map/ppermute | solution.py:496
  21.2 4.3 %collective-permute-start.6 = (bf16[8,768]{1,0:T(8,128)(2,1)S(1)}, bf16[8,768]{1,0:T(8,128)(2,1)S(1)}, u32[]{:S(2)}, u32[]{:S(2)}) collective-permute-start(bf16[8,768]{1,0:T(8,128)(2,1)S(1)} %pad_maximum_fusion.1), channel_id=1, source_target_pairs={{0,2},{1,3},{2,0},{3,1},{4,6},{5,7},{6,4},{7,5},{8,10},{9,11},{10,... | collective-permute-start | bytes 36872 | tf_op jit(solution)/shard_map/ppermute | solution.py:48
  25.5 1.8 %own_norm.1.xq_ref.refs_8_ = bf16[1024,768]{1,0:T(8,128)(2,1)S(1)} custom-call(bf16[32,32,768]{2,1,0:T(8,128)(2,1)S(1)} %copy-done), custom_call_target="tpu_custom_call" | custom-call | flops 10000000 | bytes 3000000 | tf_op jit(solution)/shard_map/own_norm/pallas_call | solution.py:508
  27.3 0.0 copy-start.4
  27.3 0.0 collective-permute-done.6
  27.3 2.6 %halo_norm.1 = (bf16[1600,768]{1,0:T(8,128)(2,1)S(1)}, f32[16,8,256]{2,1,0:T(8,128)S(1)}) custom-call(s32[10]{0:T(128)S(1)} %stack.63.place_ref, bf16[1024,768]{1,0:T(8,128)(2,1)S(1)} %own_norm.1.xq_ref.refs_8_, bf16[32,32,128]{2,1,0:T(8,128)(2,1)S(1)} %get-tuple-element.27.mark_ref, bf16[4,32,768]{2,1,0:T(8,128)(2,1)S(1)} %collective-permute-done.2.even_rows_ref, ...), custom_call_target="tpu_custom_call" | custom-call | flops 10000000 | bytes 6000000 | tf_op jit(solution)/shard_map/halo_norm/pallas_call | solution.py:517
  29.9 2.7 %collective-permute-start.7 = (bf16[192,768]{1,0:T(8,128)(2,1)}, bf16[192,768]{1,0:T(8,128)(2,1)S(1)}, u32[]{:S(2)}, u32[]{:S(2)}) collective-permute-start(bf16[192,768]{1,0:T(8,128)(2,1)} %collective-permute-done.1.refs_2_), channel_id=1, source_target_pairs={{0,4},{4,0},{8,12},{12,8},{1,5},{5,1},{9,13},{13,9},{2,6},{6,2},{1... | collective-permute-start | bytes 884744 | tf_op jit(solution)/shard_map/ppermute | solution.py:48
  32.7 0.1 collective-permute-start.11
  32.7 0.0 collective-permute-done.8.refs_4_
  32.7 0.4 collective-permute-start.9
  33.2 2.9 %collective-permute-start.13 = (bf16[208,768]{1,0:T(8,128)(2,1)S(1)}, bf16[208,768]{1,0:T(8,128)(2,1)S(1)}, u32[]{:S(2)}, u32[]{:S(2)}) collective-permute-start(bf16[208,768]{1,0:T(8,128)(2,1)S(1)} %pad_maximum_fusion.refs_0_), channel_id=1, source_target_pairs={{0,8},{4,12},{8,0},{12,4},{1,9},{5,13},{9,1},{13,5},{2,10},{6,14},... | collective-permute-start | bytes 958472 | tf_op jit(solution)/shard_map/ppermute | solution.py:48
  36.1 0.2 collective-permute-start.12
  36.3 8.9 %project.1 = (bf16[3,1024,256]{2,1,0:T(8,128)(2,1)S(1)}, bf16[3,1600,256]{2,1,0:T(8,128)(2,1)S(1)}, bf16[6,1600,256]{2,1,0:T(8,128)(2,1)S(1)}, bf16[2304,768]{1,0:T(8,128)(2,1)S(1)}) custom-call(s32[10]{0:T(128)S(1)} %stack.63.place_ref, bf16[576,768]{1,0:T(8,128)(2,1)S(1)} %bitcast.15, bf16[576,768]{1,0:T(8,128)(2,1)} %collective-permute-done.refs_1_, ...), custom_call_target="tpu_custom_call" | custom-call | flops 5000000000 | bytes 14000000 | tf_op jit(solution)/shard_map/project/pallas_call | solution.py:546
  45.2 0.4 collective-permute-start.14
  45.6 1.3 %collective-permute-done.14.refs_3_ = bf16[208,768]{1,0:T(8,128)(2,1)S(1)} collective-permute-done((bf16[208,768]{1,0:T(8,128)(2,1)S(1)}, bf16[208,768]{1,0:T(8,128)(2,1)S(1)}, u32[]{:S(2)}, u32[]{:S(2)}) %collective-permute-start.14) | collective-permute-done | bytes 319520 | tf_op jit(solution)/shard_map/ppermute | solution.py:48
  46.9 3.9 %carriers.1 = (bf16[2,2,768]{2,1,0:T(2,128)(2,1)}, bf16[768,768]{1,0:T(8,128)(2,1)S(1)}, bf16[12,256,256]{2,1,0:T(8,128)(2,1)S(1)}, f32[8,768]{1,0:T(8,128)S(1)}) custom-call(s32[10]{0:T(128)S(1)} %stack.63.place_ref, bf16[2304,768]{1,0:T(8,128)(2,1)S(1)} %get-tuple-element.44.wt, bf16[208,768]{1,0:T(8,128)(2,1)S(1)} %pad_maximum_fusion.refs_0_, ...), custom_call_target="tpu_custom_call" | custom-call | flops 500000000 | bytes 5000000 | tf_op jit(solution)/shard_map/carriers/pallas_call | solution.py:567
  50.8 13.4 %attend.1 = bf16[32,32,768]{2,1,0:T(8,128)(2,1)} custom-call(bf16[32,32,768]{2,1,0:T(8,128)(2,1)S(1)} %copy-done, bf16[3,1024,256]{2,1,0:T(8,128)(2,1)S(1)} %get-tuple-element.40.q_s, bf16[3,1600,256]{2,1,0:T(8,128)(2,1)S(1)} %get-tuple-element.41.k_s, bf16[6,1600,256]{2,1,0:T(8,128)(2,1)S(1)} %get-tuple-element.42.v_s, ...), custom_call_target="tpu_custom_call" | custom-call | flops 5000000000 | bytes 12000000 | tf_op jit(solution)/shard_map/attend/pallas_call | solution.py:586
  (20 shorter events, 0.1 us)
Async XLA Ops:
  0.6 8.5 %copy-start = (bf16[32,32,768]{2,1,0:T(8,128)(2,1)S(1)}, bf16[32,32,768]{2,1,0:T(8,128)(2,1)}, u32[]{:S(2)}) copy-start(bf16[32,32,768]{2,1,0:T(8,128)(2,1)} %x_ref.5) | copy-start | bytes 4718596
  0.6 8.5 %copy-start.2 = (bf16[2,2,768]{2,1,0:T(2,128)(2,1)S(1)}, bf16[2,2,768]{2,1,0:T(2,128)(2,1)}, u32[]{:S(2)}) copy-start(bf16[2,2,768]{2,1,0:T(2,128)(2,1)} %carriers_ref.1) | copy-start | bytes 18436
  3.4 0.7 %copy-start.3 = (bf16[192,768]{1,0:T(8,128)(2,1)}, bf16[192,768]{1,0:T(8,128)(2,1)S(1)}, u32[]{:S(2)}) copy-start(bf16[192,768]{1,0:T(8,128)(2,1)S(1)} %get-tuple-element.38) | copy-start | bytes 884740
  4.1 10.2 %copy-start.1 = (bf16[768,576]{0,1:T(8,128)(2,1)S(1)}, bf16[768,576]{0,1:T(8,128)(2,1)}, u32[]{:S(2)}) copy-start(bf16[768,576]{0,1:T(8,128)(2,1)} %param.7) | copy-start | bytes 2654212
  4.1 5.1 %collective-permute-start.2 = (bf16[4,32,768]{2,1,0:T(8,128)(2,1)S(1)}, bf16[4,32,768]{2,1,0:T(8,128)(2,1)S(1)}, u32[]{:S(2)}, u32[]{:S(2)}) collective-permute-start(bf16[4,32,768]{2,1,0:T(8,128)(2,1)S(1)} %get-tuple-element.28), channel_id=1, source_target_pairs={{0,4},{8,12},{4,0},{12,8},{1,5},{9,13},{5,1},{13,9},{2,6},{10,14},... | collective-permute-start | bytes 589832 | tf_op jit(solution)/shard_map/ppermute | solution.py:42
  4.5 4.6 %collective-permute-start.3 = (bf16[4,32,768]{2,1,0:T(8,128)(2,1)S(1)}, bf16[4,32,768]{2,1,0:T(8,128)(2,1)S(1)}, u32[]{:S(2)}, u32[]{:S(2)}) collective-permute-start(bf16[4,32,768]{2,1,0:T(8,128)(2,1)S(1)} %get-tuple-element.29), channel_id=1, source_target_pairs={{4,8},{8,4},{5,9},{9,5},{6,10},{10,6},{7,11},{11,7},{20,24},{24,20... | collective-permute-start | bytes 589832 | tf_op jit(solution)/shard_map/ppermute | solution.py:42
  5.2 14.4 %collective-permute-start.1 = (bf16[192,768]{1,0:T(8,128)(2,1)}, bf16[192,768]{1,0:T(8,128)(2,1)}, u32[]{:S(2)}, u32[]{:S(2)}) collective-permute-start(bf16[192,768]{1,0:T(8,128)(2,1)} %get-tuple-element.26), channel_id=1, source_target_pairs={{0,8},{4,12},{8,0},{12,4},{1,9},{5,13},{9,1},{13,5},{2,10},{6,14},... | collective-permute-start | bytes 884744 | tf_op jit(solution)/shard_map/ppermute | solution.py:48
  10.9 8.7 %collective-permute-start.4 = (bf16[21,8,768]{2,1,0:T(8,128)(2,1)}, bf16[21,8,768]{2,1,0:T(8,128)(2,1)S(1)}, u32[]{:S(2)}, u32[]{:S(2)}) collective-permute-start(bf16[21,8,768]{2,1,0:T(8,128)(2,1)} %get-tuple-element.30), channel_id=1, source_target_pairs={{0,1},{2,3},{1,0},{3,2},{4,5},{6,7},{5,4},{7,6},{8,9},{10,11},{9,8... | collective-permute-start | bytes 774152 | tf_op jit(solution)/shard_map/ppermute | solution.py:42
  12.9 6.7 %collective-permute-start.5 = (bf16[20,8,768]{2,1,0:T(8,128)(2,1)}, bf16[20,8,768]{2,1,0:T(8,128)(2,1)}, u32[]{:S(2)}, u32[]{:S(2)}) collective-permute-start(bf16[20,8,768]{2,1,0:T(8,128)(2,1)} %get-tuple-element.31), channel_id=1, source_target_pairs={{1,2},{2,1},{5,6},{6,5},{9,10},{10,9},{13,14},{14,13},{17,18},{18,... | collective-permute-start | bytes 737288 | tf_op jit(solution)/shard_map/ppermute | solution.py:42
  14.3 22.0 %collective-permute-start = (bf16[576,768]{1,0:T(8,128)(2,1)S(1)}, bf16[576,768]{1,0:T(8,128)(2,1)}, u32[]{:S(2)}, u32[]{:S(2)}) collective-permute-start(bf16[576,768]{1,0:T(8,128)(2,1)S(1)} %bitcast.14), channel_id=1, source_target_pairs={{0,4},{4,0},{8,12},{12,8},{1,5},{5,1},{9,13},{13,9},{2,6},{6,2},{1... | collective-permute-start | bytes 2654216 | tf_op jit(solution)/shard_map/ppermute | solution.py:48
  18.5 14.2 %collective-permute-start.10 = (bf16[192,768]{1,0:T(8,128)(2,1)}, bf16[192,768]{1,0:T(8,128)(2,1)S(1)}, u32[]{:S(2)}, u32[]{:S(2)}) collective-permute-start(bf16[192,768]{1,0:T(8,128)(2,1)} %copy-done.3), channel_id=1, source_target_pairs={{0,8},{4,12},{8,0},{12,4},{1,9},{5,13},{9,1},{13,5},{2,10},{6,14},... | collective-permute-start | bytes 884744 | tf_op jit(solution)/shard_map/ppermute | solution.py:48
  19.6 13.2 %collective-permute-start.8 = (bf16[192,768]{1,0:T(8,128)(2,1)}, bf16[192,768]{1,0:T(8,128)(2,1)S(1)}, u32[]{:S(2)}, u32[]{:S(2)}) collective-permute-start(bf16[192,768]{1,0:T(8,128)(2,1)} %collective-permute-done.1.refs_2_), channel_id=1, source_target_pairs={{0,16},{16,0},{1,17},{17,1},{2,18},{18,2},{3,19},{19,3},{4,20},{20... | collective-permute-start | bytes 884744 | tf_op jit(solution)/shard_map/ppermute | solution.py:496
  21.2 6.1 %collective-permute-start.6 = (bf16[8,768]{1,0:T(8,128)(2,1)S(1)}, bf16[8,768]{1,0:T(8,128)(2,1)S(1)}, u32[]{:S(2)}, u32[]{:S(2)}) collective-permute-start(bf16[8,768]{1,0:T(8,128)(2,1)S(1)} %pad_maximum_fusion.1), channel_id=1, source_target_pairs={{0,2},{1,3},{2,0},{3,1},{4,6},{5,7},{6,4},{7,5},{8,10},{9,11},{10,... | collective-permute-start | bytes 36872 | tf_op jit(solution)/shard_map/ppermute | solution.py:48
  27.3 5.9 %copy-start.4 = (bf16[768,192]{0,1:T(8,128)(2,1)S(1)}, bf16[768,192]{0,1:T(8,128)(2,1)}, u32[]{:S(2)}) copy-start(bf16[768,192]{0,1:T(8,128)(2,1)} %param.8) | copy-start | bytes 884740
  29.9 6.2 %collective-permute-start.7 = (bf16[192,768]{1,0:T(8,128)(2,1)}, bf16[192,768]{1,0:T(8,128)(2,1)S(1)}, u32[]{:S(2)}, u32[]{:S(2)}) collective-permute-start(bf16[192,768]{1,0:T(8,128)(2,1)} %collective-permute-done.1.refs_2_), channel_id=1, source_target_pairs={{0,4},{4,0},{8,12},{12,8},{1,5},{5,1},{9,13},{13,9},{2,6},{6,2},{1... | collective-permute-start | bytes 884744 | tf_op jit(solution)/shard_map/ppermute | solution.py:48
  32.7 3.6 %collective-permute-start.11 = (bf16[192,768]{1,0:T(8,128)(2,1)S(1)}, bf16[192,768]{1,0:T(8,128)(2,1)S(1)}, u32[]{:S(2)}, u32[]{:S(2)}) collective-permute-start(bf16[192,768]{1,0:T(8,128)(2,1)S(1)} %collective-permute-done.10.refs_6_), channel_id=1, source_target_pairs={{0,4},{4,0},{8,12},{12,8},{1,5},{5,1},{9,13},{13,9},{2,6},{6,2},{1... | collective-permute-start | bytes 884744 | tf_op jit(solution)/shard_map/ppermute | solution.py:48
  32.7 3.6 %collective-permute-start.9 = (bf16[192,768]{1,0:T(8,128)(2,1)S(1)}, bf16[192,768]{1,0:T(8,128)(2,1)S(1)}, u32[]{:S(2)}, u32[]{:S(2)}) collective-permute-start(bf16[192,768]{1,0:T(8,128)(2,1)S(1)} %collective-permute-done.8.refs_4_), channel_id=1, source_target_pairs={{0,4},{4,0},{8,12},{12,8},{1,5},{5,1},{9,13},{13,9},{2,6},{6,2},{1... | collective-permute-start | bytes 884744 | tf_op jit(solution)/shard_map/ppermute | solution.py:48
  33.2 12.0 %collective-permute-start.13 = (bf16[208,768]{1,0:T(8,128)(2,1)S(1)}, bf16[208,768]{1,0:T(8,128)(2,1)S(1)}, u32[]{:S(2)}, u32[]{:S(2)}) collective-permute-start(bf16[208,768]{1,0:T(8,128)(2,1)S(1)} %pad_maximum_fusion.refs_0_), channel_id=1, source_target_pairs={{0,8},{4,12},{8,0},{12,4},{1,9},{5,13},{9,1},{13,5},{2,10},{6,14},... | collective-permute-start | bytes 958472 | tf_op jit(solution)/shard_map/ppermute | solution.py:48
  36.1 9.5 %collective-permute-start.12 = (bf16[208,768]{1,0:T(8,128)(2,1)S(1)}, bf16[208,768]{1,0:T(8,128)(2,1)S(1)}, u32[]{:S(2)}, u32[]{:S(2)}) collective-permute-start(bf16[208,768]{1,0:T(8,128)(2,1)S(1)} %pad_maximum_fusion.refs_0_), channel_id=1, source_target_pairs={{0,4},{4,0},{8,12},{12,8},{1,5},{5,1},{9,13},{13,9},{2,6},{6,2},{1... | collective-permute-start | bytes 958472 | tf_op jit(solution)/shard_map/ppermute | solution.py:48
  45.2 1.7 %collective-permute-start.14 = (bf16[208,768]{1,0:T(8,128)(2,1)S(1)}, bf16[208,768]{1,0:T(8,128)(2,1)S(1)}, u32[]{:S(2)}, u32[]{:S(2)}) collective-permute-start(bf16[208,768]{1,0:T(8,128)(2,1)S(1)} %collective-permute-done.13.refs_2_), channel_id=1, source_target_pairs={{0,4},{4,0},{8,12},{12,8},{1,5},{5,1},{9,13},{13,9},{2,6},{6,2},{1... | collective-permute-start | bytes 958472 | tf_op jit(solution)/shard_map/ppermute | solution.py:48
where the time goes:
time: 64.4 us; the launch traced here: 64.2 us
  Pallas kernels  34.8 us (54%)
  starting transfers between devices  26.4 us (41%)
  waiting for transfers between devices  1.3 us (2%)
  local copies, waits for them, and re-layouts  0.82 us (1%)
  between operations  0.81 us (1%)
    ppermute x10, starting transfers between devices, swapped(): return lax.ppermute(block, axis, [(i, i ^ bit) for i in range(count)])  20.3 us
    pallas_call x1, Pallas kernels, local(): pl.pallas_call(attend_kernel, out_shape=jax.ShapeDtypeStruct(grid_element...  13.4 us
    pallas_call x1, Pallas kernels, local(): pl.pallas_call(functools.partial(project_kernel, offsets, numbered, tripl...  8.9 us
    ppermute x4, starting transfers between devices, pair_swapped(): got.append(lax.ppermute(block, axis, pairs + [(b, a) for a, b in pairs]))  4.53 us
    pallas_call x1, Pallas kernels, local(): pl.pallas_call(functools.partial(carrier_kernel, offsets), out_shape=(jax...  3.85 us
    pallas_call x1, Pallas kernels, local(): pl.pallas_call(halo_kernel, out_shape=(jax.ShapeDtypeStruct((wide_rows *...  2.59 us
    pallas_call x1, Pallas kernels, local(): pl.pallas_call(functools.partial(edge_kernel, piece_rows), out_shape=(jax...  2.56 us
    pallas_call x1, Pallas kernels, local(): pl.pallas_call(own_kernel, out_shape=jax.ShapeDtypeStruct((rows * cols, c...  1.81 us
  transfers between devices with their start and end apart: 15, of which 1 were waited for; matrix products, arithmetic and copies ran while one was open for 0% of the time, Pallas kernels for 23%

commit v1 on v0

--- a/solution.py
+++ b/solution.py
@@ -351,12 +351,12 @@
             kce[w * groups + g] = jnp.where(same, fresh[w : w + 1, g * GROUP : (g + 1) * GROUP], 0.0).astype(jnp.bfloat16)
 
 
-def attend_kernel(x_ref, q_s, k_s, v_s, hide_ref, kce, vc_s, wo, out_hbm, out_ref, mix_s, out_sems):
-    rows, cols, channels = x_ref.shape
-    groups = channels // GROUP
+def attend_kernel(tall, broad, q_s, k_s, v_s, hide_ref, kce, vc_s, mix_s, pc_s, even_s, odd_s):
+    groups, tiles = q_s.shape[0], hide_ref.shape[0]
     heads_in = GROUP // HEAD_DIM
-    wide_rows = rows + 2 * RADIUS
     queries, span = TILE * TILE, 2 * TILE * TILE
+    side = PATCH_SIDE // TILE
+    wide = (tall + 1) * queries
     qi = lax.broadcasted_iota(jnp.int32, (queries, 2 * span), 0)
     ki = lax.broadcasted_iota(jnp.int32, (queries, 2 * span), 1)
     row_step = (ki % span) // TILE - qi // TILE
@@ -365,47 +365,70 @@
     band = jnp.where(seen, 0.0, HIDDEN)
     group_head = lax.broadcasted_iota(jnp.int32, (1, GROUP), 1) // HEAD_DIM
     only = [jnp.where(group_head == h, 1.0, 0.0).astype(jnp.bfloat16) for h in range(heads_in)]
-    pair_head = lax.broadcasted_iota(jnp.int32, (1, LANES), 1) // HEAD_DIM
     pairs, in_pair = GROUP // LANES, LANES // HEAD_DIM
-    tall, broad = rows // TILE, cols // TILE
-    per_side = PATCH_SIDE // TILE
-
-    def tile(t, _):
-        c, r = t // tall, t % tall
-        q_at = pl.multiple_of(c * (rows * TILE) + r * queries, queries)
-        k0 = pl.multiple_of(c * (wide_rows * TILE) + r * queries, queries)
-        k1 = pl.multiple_of(k0 + wide_rows * TILE, queries)
-        window = (r // per_side) * (broad // per_side) + c // per_side
-        bias = band + hide_ref[t][0:1, :]
+    pair_head = lax.broadcasted_iota(jnp.int32, (1, 2 * LANES), 1) % LANES // HEAD_DIM
+
+    for c in range(broad):
+        for w in range(tall // side):
+            at = slice((c * tall + w * side) * queries, (c * tall + (w + 1) * side) * queries)
+            window = w * (broad // side) + c // side
+            for g in range(groups):
+                pc_s[at, g * GROUP : (g + 1) * GROUP] = jnp.exp2(nt(q_s[g, at, :], kce[window * groups + g]))
+
+    def keys_at(t):
+        k0 = pl.multiple_of(t // tall * wide + t % tall * queries, queries)
+        return k0, pl.multiple_of(k0 + wide, queries)
+
+    def scores(t, ref):
+        q_at = pl.multiple_of(t * queries, queries)
+        k0, k1 = keys_at(t)
         for g in range(groups):
             q = q_s[g, pl.ds(q_at, queries), :]
             qq = jnp.concatenate([q * mask for mask in only], axis=0)
             k = jnp.concatenate([k_s[g, pl.ds(k0, span), :], k_s[g, pl.ds(k1, span), :]], axis=0)
-            p = jnp.exp2(nt(qq, k).reshape(heads_in, queries, 2 * span) + bias[None])
+            ref[g] = nt(qq, k)
+
+    def finish(t, ref):
+        q_at = pl.multiple_of(t * queries, queries)
+        k0, k1 = keys_at(t)
+        window = t % tall // side * (broad // side) + t // tall // side
+        bias = band + hide_ref[t][0:1, :]
+        for g in range(groups):
+            p = jnp.exp2(ref[g].reshape(heads_in, queries, 2 * span) + bias[None])
             p = p.reshape(heads_in * queries, 2 * span).astype(jnp.bfloat16)
-            pc = jnp.exp2(nt(q, kce[window * groups + g]))
             v_new = vc_s[pl.ds(window, 1), g * GROUP : (g + 1) * GROUP]
             for j in range(pairs):
+                at = slice(g * GROUP + j * LANES, g * GROUP + (j + 1) * LANES)
                 v = jnp.concatenate(
                     [v_s[pairs * g + j, pl.ds(k0, span), :], v_s[pairs * g + j, pl.ds(k1, span), :]], axis=0
                 )
                 o = nn(p[j * in_pair * queries : (j + 1) * in_pair * queries, :], v)
                 kept = o[:queries]
                 for h in range(1, in_pair):
-                    mine = o[h * queries : (h + 1) * queries]
-                    kept = jnp.where(jnp.concatenate([pair_head] * 2, axis=1) == h, mine, kept)
-                new = pc[:, j * LANES : (j + 1) * LANES]
-                at = slice(g * GROUP + j * LANES, g * GROUP + (j + 1) * LANES)
+                    kept = jnp.where(pair_head == h, o[h * queries : (h + 1) * queries], kept)
+                new = pc_s[pl.ds(q_at, queries), at]
                 mixed = (kept[:, :LANES] + new * v_new[:, j * LANES : (j + 1) * LANES]) / (kept[:, LANES:] + new)
                 mix_s[pl.ds(q_at, queries), at] = mixed.astype(jnp.bfloat16)
+
+    scores(0, even_s)
+
+    def two(i, _):
+        t = 2 * i
+        scores(t + 1, odd_s)
+        finish(t, even_s)
+        scores(jnp.minimum(t + 2, tiles - 1), even_s)
+        finish(t + 1, odd_s)
         return 0
 
-    lax.fori_loop(0, tall * broad, tile, 0, unroll=2)
-
+    lax.fori_loop(0, tiles // 2, two, 0)
+
+
+def out_kernel(x_ref, mix_s, wo, out_hbm, out_ref, out_sems):
+    rows, cols, channels = x_ref.shape
     going = []
-    for pair in range(broad // 2):
+    for pair in range(cols // (2 * TILE)):
         both = slice(2 * pair * TILE, 2 * (pair + 1) * TILE)
-        for g in range(groups):
+        for g in range(channels // GROUP):
             at = slice(g * GROUP, (g + 1) * GROUP)
             w = wo[at, :]
             parts = [
@@ -583,20 +606,35 @@
         name="carriers",
     )(place, wt, *finals)
 
+    scores = (groups, GROUP // HEAD_DIM * TILE * TILE, keys)
+    mix = pl.pallas_call(
+        functools.partial(attend_kernel, rows // TILE, cols // TILE),
+        out_shape=jax.ShapeDtypeStruct((rows * cols, channels), jnp.bfloat16),
+        in_specs=[vmem] * 6,
+        out_specs=vmem,
+        scratch_shapes=[
+            pltpu.VMEM((rows * cols, channels), jnp.float32),
+            pltpu.VMEM(scores, jnp.float32),
+            pltpu.VMEM(scores, jnp.float32),
+        ],
+        compiler_params=pltpu.CompilerParams(vmem_limit_bytes=VMEM_BYTES),
+        cost_estimate=pl.CostEstimate(flops=4_000_000_000, bytes_accessed=12_000_000, transcendentals=4_000_000),
+        name="attend",
+    )(q, k, v, hide, kce, vc)
+
     out = pl.pallas_call(
-        attend_kernel,
+        out_kernel,
         out_shape=jax.ShapeDtypeStruct(grid_elements.shape, jnp.bfloat16),
-        in_specs=[vmem] * 8,
+        in_specs=[vmem] * 3,
         out_specs=anywhere,
         scratch_shapes=[
             pltpu.VMEM((cols // (2 * TILE), rows, 2 * TILE, channels), jnp.bfloat16),
-            pltpu.VMEM((rows * cols, channels), jnp.bfloat16),
             pltpu.SemaphoreType.DMA((cols // (2 * TILE),)),
         ],
         compiler_params=pltpu.CompilerParams(vmem_limit_bytes=VMEM_BYTES),
-        cost_estimate=pl.CostEstimate(flops=5_000_000_000, bytes_accessed=12_000_000, transcendentals=4_000_000),
-        name="attend",
-    )(grid_elements, q, k, v, hide, kce, vc, wo)
+        cost_estimate=pl.CostEstimate(flops=1_200_000_000, bytes_accessed=6_000_000, transcendentals=0),
+        name="out",
+    )(grid_elements, mix, wo)
     return (out, summary_result)
 
 

time: 64.4 us -> 60.2 us (0.935)
  Pallas kernels: 34.8 us -> 30.6 us
    pallas_call x1 -> x2, Pallas kernels: 13.4 us -> 9.22 us  [the longest x1 6.85 us: local(): pl.pallas_call(functools.partial(attend_kernel, rows // TILE, cols // TIL...]
  transfers between devices with their start and end apart: 15 -> 15, of which waited for: 1 -> 1; matrix products, arithmetic and copies ran while one was open for 0% -> 0% of each run, Pallas kernels for 23% -> 25%
where the time goes in v1:
time: 60.2 us; the launch traced here: 60 us
  Pallas kernels  30.6 us (51%)
  starting transfers between devices  26.4 us (44%)
  waiting for transfers between devices  1.3 us (2%)
  local copies, waits for them, and re-layouts  0.82 us (1%)
  between operations  0.82 us (1%)
    ppermute x10, starting transfers between devices, swapped(): return lax.ppermute(block, axis, [(i, i ^ bit) for i in range(count)])  20.3 us
    pallas_call x1, Pallas kernels, local(): pl.pallas_call(functools.partial(project_kernel, offsets, numbered, tripl...  8.9 us
    pallas_call x1, Pallas kernels, local(): pl.pallas_call(functools.partial(attend_kernel, rows // TILE, cols // TIL...  6.85 us
    ppermute x4, starting transfers between devices, pair_swapped(): got.append(lax.ppermute(block, axis, pairs + [(b, a) for a, b in pairs]))  4.53 us
    pallas_call x1, Pallas kernels, local(): pl.pallas_call(functools.partial(carrier_kernel, offsets), out_shape=(jax...  3.85 us
    pallas_call x1, Pallas kernels, local(): pl.pallas_call(halo_kernel, out_shape=(jax.ShapeDtypeStruct((wide_rows *...  2.59 us
    pallas_call x1, Pallas kernels, local(): pl.pallas_call(functools.partial(edge_kernel, piece_rows), out_shape=(jax...  2.56 us
    pallas_call x1, Pallas kernels, local(): pl.pallas_call(out_kernel, out_shape=jax.ShapeDtypeStruct(grid_elements.s...  2.37 us
  transfers between devices with their start and end apart: 15, of which 1 were waited for; matrix products, arithmetic and copies ran while one was open for 0% of the time, Pallas kernels for 25%

profile of v1, /device:TPU:0, one launch (start us, length us, event | category | flops | bytes accessed | tf_op | source)
XLA Modules:
  0.0 60.0 jit_solution(3120639085367611045)
XLA Ops:
  0.6 0.0 copy-start
  0.7 0.1 stack.63.place_ref
  0.8 2.6 %edge_rows.1 = (bf16[32,32,128]{2,1,0:T(8,128)(2,1)S(1)}, bf16[4,32,768]{2,1,0:T(8,128)(2,1)S(1)}, bf16[4,32,768]{2,1,0:T(8,128)(2,1)S(1)}, bf16[192,768]{1,0:T(8,128)(2,1)}, bf16[192,768]{1,0:T(8,128)(2,1)S(1)}) custom-call(s32[10]{0:T(128)S(1)} %stack.63.place_ref, s32[32,32]{1,0:T(8,128)} %flags_hbm.1, bf16[32,32,768]{2,1,0:T(8,128)(2,1)} %x_ref.5, ...), custom_call_target="tpu_custom_call" | custom-call | flops 1000000 | bytes 2000000 | tf_op jit(solution)/shard_map/edge_rows/pallas_call | solution.py:471
  3.4 0.7 %copy-done.3 = bf16[192,768]{1,0:T(8,128)(2,1)} copy-done((bf16[192,768]{1,0:T(8,128)(2,1)}, bf16[192,768]{1,0:T(8,128)(2,1)S(1)}, u32[]{:S(2)}) %copy-start.3) | copy-done | bytes 294936
  4.1 0.5 collective-permute-start.2
  4.5 0.7 %collective-permute-start.3 = (bf16[4,32,768]{2,1,0:T(8,128)(2,1)S(1)}, bf16[4,32,768]{2,1,0:T(8,128)(2,1)S(1)}, u32[]{:S(2)}, u32[]{:S(2)}) collective-permute-start(bf16[4,32,768]{2,1,0:T(8,128)(2,1)S(1)} %get-tuple-element.29), channel_id=1, source_target_pairs={{4,8},{8,4},{5,9},{9,5},{6,10},{10,6},{7,11},{11,7},{20,24},{24,20... | collective-permute-start | bytes 589832 | tf_op jit(solution)/shard_map/ppermute | solution.py:42
  5.2 4.0 %collective-permute-start.1 = (bf16[192,768]{1,0:T(8,128)(2,1)}, bf16[192,768]{1,0:T(8,128)(2,1)}, u32[]{:S(2)}, u32[]{:S(2)}) collective-permute-start(bf16[192,768]{1,0:T(8,128)(2,1)} %get-tuple-element.26), channel_id=1, source_target_pairs={{0,8},{4,12},{8,0},{12,4},{1,9},{5,13},{9,1},{13,5},{2,10},{6,14},... | collective-permute-start | bytes 884744 | tf_op jit(solution)/shard_map/ppermute | solution.py:48
  9.2 0.0 collective-permute-done.2.even_rows_ref
  9.2 0.0 collective-permute-done.3.odd_rows_ref
  9.2 1.7 %edge_columns.1 = (bf16[21,8,768]{2,1,0:T(8,128)(2,1)}, bf16[20,8,768]{2,1,0:T(8,128)(2,1)}) custom-call(s32[10]{0:T(128)S(1)} %stack.63.place_ref, bf16[32,32,768]{2,1,0:T(8,128)(2,1)S(1)} %copy-done, bf16[32,32,128]{2,1,0:T(8,128)(2,1)S(1)} %get-tuple-element.27.mark_ref, bf16[4,32,768]{2,1,0:T(8,128)(2,1)S(1)} %collective-permute-done.2.even_rows_ref, ...), custom_call_target="tpu_custom_call" | custom-call | flops 1000000 | bytes 2000000 | tf_op jit(solution)/shard_map/edge_columns/pallas_call | solution.py:501
  10.9 2.1 %collective-permute-start.4 = (bf16[21,8,768]{2,1,0:T(8,128)(2,1)}, bf16[21,8,768]{2,1,0:T(8,128)(2,1)S(1)}, u32[]{:S(2)}, u32[]{:S(2)}) collective-permute-start(bf16[21,8,768]{2,1,0:T(8,128)(2,1)} %get-tuple-element.30), channel_id=1, source_target_pairs={{0,1},{2,3},{1,0},{3,2},{4,5},{6,7},{5,4},{7,6},{8,9},{10,11},{9,8... | collective-permute-start | bytes 774152 | tf_op jit(solution)/shard_map/ppermute | solution.py:42
  12.9 1.4 %collective-permute-start.5 = (bf16[20,8,768]{2,1,0:T(8,128)(2,1)}, bf16[20,8,768]{2,1,0:T(8,128)(2,1)}, u32[]{:S(2)}, u32[]{:S(2)}) collective-permute-start(bf16[20,8,768]{2,1,0:T(8,128)(2,1)} %get-tuple-element.31), channel_id=1, source_target_pairs={{1,2},{2,1},{5,6},{6,5},{9,10},{10,9},{13,14},{14,13},{17,18},{18,... | collective-permute-start | bytes 737288 | tf_op jit(solution)/shard_map/ppermute | solution.py:42
  14.3 4.2 %collective-permute-start = (bf16[576,768]{1,0:T(8,128)(2,1)S(1)}, bf16[576,768]{1,0:T(8,128)(2,1)}, u32[]{:S(2)}, u32[]{:S(2)}) collective-permute-start(bf16[576,768]{1,0:T(8,128)(2,1)S(1)} %bitcast.14), channel_id=1, source_target_pairs={{0,4},{4,0},{8,12},{12,8},{1,5},{5,1},{9,13},{13,9},{2,6},{6,2},{1... | collective-permute-start | bytes 2654216 | tf_op jit(solution)/shard_map/ppermute | solution.py:48
  18.5 1.1 %collective-permute-start.10 = (bf16[192,768]{1,0:T(8,128)(2,1)}, bf16[192,768]{1,0:T(8,128)(2,1)S(1)}, u32[]{:S(2)}, u32[]{:S(2)}) collective-permute-start(bf16[192,768]{1,0:T(8,128)(2,1)} %copy-done.3), channel_id=1, source_target_pairs={{0,8},{4,12},{8,0},{12,4},{1,9},{5,13},{9,1},{13,5},{2,10},{6,14},... | collective-permute-start | bytes 884744 | tf_op jit(solution)/shard_map/ppermute | solution.py:48
  19.6 0.0 collective-permute-done.4.even_cols_ref
  19.6 1.6 %collective-permute-start.8 = (bf16[192,768]{1,0:T(8,128)(2,1)}, bf16[192,768]{1,0:T(8,128)(2,1)S(1)}, u32[]{:S(2)}, u32[]{:S(2)}) collective-permute-start(bf16[192,768]{1,0:T(8,128)(2,1)} %collective-permute-done.1.refs_2_), channel_id=1, source_target_pairs={{0,16},{16,0},{1,17},{17,1},{2,18},{18,2},{3,19},{19,3},{4,20},{20... | collective-permute-start | bytes 884744 | tf_op jit(solution)/shard_map/ppermute | solution.py:519
  21.2 4.3 %collective-permute-start.6 = (bf16[8,768]{1,0:T(8,128)(2,1)S(1)}, bf16[8,768]{1,0:T(8,128)(2,1)S(1)}, u32[]{:S(2)}, u32[]{:S(2)}) collective-permute-start(bf16[8,768]{1,0:T(8,128)(2,1)S(1)} %pad_maximum_fusion.1), channel_id=1, source_target_pairs={{0,2},{1,3},{2,0},{3,1},{4,6},{5,7},{6,4},{7,5},{8,10},{9,11},{10,... | collective-permute-start | bytes 36872 | tf_op jit(solution)/shard_map/ppermute | solution.py:48
  25.5 1.8 %own_norm.1.xq_ref.refs_8_ = bf16[1024,768]{1,0:T(8,128)(2,1)S(1)} custom-call(bf16[32,32,768]{2,1,0:T(8,128)(2,1)S(1)} %copy-done), custom_call_target="tpu_custom_call" | custom-call | flops 10000000 | bytes 3000000 | tf_op jit(solution)/shard_map/own_norm/pallas_call | solution.py:531
  27.3 0.0 copy-start.4
  27.3 0.0 collective-permute-done.6
  27.3 2.6 %halo_norm.1 = (bf16[1600,768]{1,0:T(8,128)(2,1)S(1)}, f32[16,8,256]{2,1,0:T(8,128)S(1)}) custom-call(s32[10]{0:T(128)S(1)} %stack.63.place_ref, bf16[1024,768]{1,0:T(8,128)(2,1)S(1)} %own_norm.1.xq_ref.refs_8_, bf16[32,32,128]{2,1,0:T(8,128)(2,1)S(1)} %get-tuple-element.27.mark_ref, bf16[4,32,768]{2,1,0:T(8,128)(2,1)S(1)} %collective-permute-done.2.even_rows_ref, ...), custom_call_target="tpu_custom_call" | custom-call | flops 10000000 | bytes 6000000 | tf_op jit(solution)/shard_map/halo_norm/pallas_call | solution.py:540
  29.9 2.7 %collective-permute-start.7 = (bf16[192,768]{1,0:T(8,128)(2,1)}, bf16[192,768]{1,0:T(8,128)(2,1)S(1)}, u32[]{:S(2)}, u32[]{:S(2)}) collective-permute-start(bf16[192,768]{1,0:T(8,128)(2,1)} %collective-permute-done.1.refs_2_), channel_id=1, source_target_pairs={{0,4},{4,0},{8,12},{12,8},{1,5},{5,1},{9,13},{13,9},{2,6},{6,2},{1... | collective-permute-start | bytes 884744 | tf_op jit(solution)/shard_map/ppermute | solution.py:48
  32.7 0.1 collective-permute-start.11
  32.7 0.4 collective-permute-start.9
  33.2 2.9 %collective-permute-start.13 = (bf16[208,768]{1,0:T(8,128)(2,1)S(1)}, bf16[208,768]{1,0:T(8,128)(2,1)S(1)}, u32[]{:S(2)}, u32[]{:S(2)}) collective-permute-start(bf16[208,768]{1,0:T(8,128)(2,1)S(1)} %pad_maximum_fusion.refs_0_), channel_id=1, source_target_pairs={{0,8},{4,12},{8,0},{12,4},{1,9},{5,13},{9,1},{13,5},{2,10},{6,14},... | collective-permute-start | bytes 958472 | tf_op jit(solution)/shard_map/ppermute | solution.py:48
  36.1 0.2 collective-permute-start.12
  36.3 8.9 %project.1 = (bf16[3,1024,256]{2,1,0:T(8,128)(2,1)S(1)}, bf16[3,1600,256]{2,1,0:T(8,128)(2,1)S(1)}, bf16[6,1600,256]{2,1,0:T(8,128)(2,1)S(1)}, bf16[2304,768]{1,0:T(8,128)(2,1)S(1)}) custom-call(s32[10]{0:T(128)S(1)} %stack.63.place_ref, bf16[576,768]{1,0:T(8,128)(2,1)S(1)} %bitcast.15, bf16[576,768]{1,0:T(8,128)(2,1)} %collective-permute-done.refs_1_, ...), custom_call_target="tpu_custom_call" | custom-call | flops 5000000000 | bytes 14000000 | tf_op jit(solution)/shard_map/project/pallas_call | solution.py:569
  45.2 0.4 collective-permute-start.14
  45.6 1.3 %collective-permute-done.14.refs_3_ = bf16[208,768]{1,0:T(8,128)(2,1)S(1)} collective-permute-done((bf16[208,768]{1,0:T(8,128)(2,1)S(1)}, bf16[208,768]{1,0:T(8,128)(2,1)S(1)}, u32[]{:S(2)}, u32[]{:S(2)}) %collective-permute-start.14) | collective-permute-done | bytes 319520 | tf_op jit(solution)/shard_map/ppermute | solution.py:48
  46.9 3.9 %carriers.1 = (bf16[2,2,768]{2,1,0:T(2,128)(2,1)}, bf16[768,768]{1,0:T(8,128)(2,1)S(1)}, bf16[12,256,256]{2,1,0:T(8,128)(2,1)S(1)}, f32[8,768]{1,0:T(8,128)S(1)}) custom-call(s32[10]{0:T(128)S(1)} %stack.63.place_ref, bf16[2304,768]{1,0:T(8,128)(2,1)S(1)} %get-tuple-element.44.wt, bf16[208,768]{1,0:T(8,128)(2,1)S(1)} %pad_maximum_fusion.refs_0_, ...), custom_call_target="tpu_custom_call" | custom-call | flops 500000000 | bytes 5000000 | tf_op jit(solution)/shard_map/carriers/pallas_call | solution.py:590
  50.8 6.9 %attend.1.mix_s = bf16[1024,768]{1,0:T(8,128)(2,1)S(1)} custom-call(bf16[3,1024,256]{2,1,0:T(8,128)(2,1)S(1)} %get-tuple-element.40.q_s, bf16[3,1600,256]{2,1,0:T(8,128)(2,1)S(1)} %get-tuple-element.41.k_s, bf16[6,1600,256]{2,1,0:T(8,128)(2,1)S(1)} %get-tuple-element.42.v_s, f32[16,8,256]{2,1,0:T(8,128)S(1)} %get-tuple-element.43.hide_ref, ...), custom_call_target="tpu_custom_call" | custom-call | flops 4000000000 | bytes 12000000 | tf_op jit(solution)/shard_map/attend/pallas_call | solution.py:610
  57.6 2.4 %out.1 = bf16[32,32,768]{2,1,0:T(8,128)(2,1)} custom-call(bf16[32,32,768]{2,1,0:T(8,128)(2,1)S(1)} %copy-done, bf16[1024,768]{1,0:T(8,128)(2,1)S(1)} %attend.1.mix_s, bf16[768,768]{1,0:T(8,128)(2,1)S(1)} %get-tuple-element.48.wo), custom_call_target="tpu_custom_call" | custom-call | flops 1200000000 | bytes 6000000 | tf_op jit(solution)/shard_map/out/pallas_call | solution.py:625
  (21 shorter events, 0.1 us)
Async XLA Ops:
  0.6 8.5 %copy-start = (bf16[32,32,768]{2,1,0:T(8,128)(2,1)S(1)}, bf16[32,32,768]{2,1,0:T(8,128)(2,1)}, u32[]{:S(2)}) copy-start(bf16[32,32,768]{2,1,0:T(8,128)(2,1)} %x_ref.5) | copy-start | bytes 4718596
  0.6 8.5 %copy-start.2 = (bf16[2,2,768]{2,1,0:T(2,128)(2,1)S(1)}, bf16[2,2,768]{2,1,0:T(2,128)(2,1)}, u32[]{:S(2)}) copy-start(bf16[2,2,768]{2,1,0:T(2,128)(2,1)} %carriers_ref.1) | copy-start | bytes 18436
  3.4 0.7 %copy-start.3 = (bf16[192,768]{1,0:T(8,128)(2,1)}, bf16[192,768]{1,0:T(8,128)(2,1)S(1)}, u32[]{:S(2)}) copy-start(bf16[192,768]{1,0:T(8,128)(2,1)S(1)} %get-tuple-element.38) | copy-start | bytes 884740
  4.1 10.2 %copy-start.1 = (bf16[768,576]{0,1:T(8,128)(2,1)S(1)}, bf16[768,576]{0,1:T(8,128)(2,1)}, u32[]{:S(2)}) copy-start(bf16[768,576]{0,1:T(8,128)(2,1)} %param.7) | copy-start | bytes 2654212
  4.1 5.1 %collective-permute-start.2 = (bf16[4,32,768]{2,1,0:T(8,128)(2,1)S(1)}, bf16[4,32,768]{2,1,0:T(8,128)(2,1)S(1)}, u32[]{:S(2)}, u32[]{:S(2)}) collective-permute-start(bf16[4,32,768]{2,1,0:T(8,128)(2,1)S(1)} %get-tuple-element.28), channel_id=1, source_target_pairs={{0,4},{8,12},{4,0},{12,8},{1,5},{9,13},{5,1},{13,9},{2,6},{10,14},... | collective-permute-start | bytes 589832 | tf_op jit(solution)/shard_map/ppermute | solution.py:42
  4.5 4.6 %collective-permute-start.3 = (bf16[4,32,768]{2,1,0:T(8,128)(2,1)S(1)}, bf16[4,32,768]{2,1,0:T(8,128)(2,1)S(1)}, u32[]{:S(2)}, u32[]{:S(2)}) collective-permute-start(bf16[4,32,768]{2,1,0:T(8,128)(2,1)S(1)} %get-tuple-element.29), channel_id=1, source_target_pairs={{4,8},{8,4},{5,9},{9,5},{6,10},{10,6},{7,11},{11,7},{20,24},{24,20... | collective-permute-start | bytes 589832 | tf_op jit(solution)/shard_map/ppermute | solution.py:42
  5.2 14.4 %collective-permute-start.1 = (bf16[192,768]{1,0:T(8,128)(2,1)}, bf16[192,768]{1,0:T(8,128)(2,1)}, u32[]{:S(2)}, u32[]{:S(2)}) collective-permute-start(bf16[192,768]{1,0:T(8,128)(2,1)} %get-tuple-element.26), channel_id=1, source_target_pairs={{0,8},{4,12},{8,0},{12,4},{1,9},{5,13},{9,1},{13,5},{2,10},{6,14},... | collective-permute-start | bytes 884744 | tf_op jit(solution)/shard_map/ppermute | solution.py:48
  10.9 8.7 %collective-permute-start.4 = (bf16[21,8,768]{2,1,0:T(8,128)(2,1)}, bf16[21,8,768]{2,1,0:T(8,128)(2,1)S(1)}, u32[]{:S(2)}, u32[]{:S(2)}) collective-permute-start(bf16[21,8,768]{2,1,0:T(8,128)(2,1)} %get-tuple-element.30), channel_id=1, source_target_pairs={{0,1},{2,3},{1,0},{3,2},{4,5},{6,7},{5,4},{7,6},{8,9},{10,11},{9,8... | collective-permute-start | bytes 774152 | tf_op jit(solution)/shard_map/ppermute | solution.py:42
  12.9 6.7 %collective-permute-start.5 = (bf16[20,8,768]{2,1,0:T(8,128)(2,1)}, bf16[20,8,768]{2,1,0:T(8,128)(2,1)}, u32[]{:S(2)}, u32[]{:S(2)}) collective-permute-start(bf16[20,8,768]{2,1,0:T(8,128)(2,1)} %get-tuple-element.31), channel_id=1, source_target_pairs={{1,2},{2,1},{5,6},{6,5},{9,10},{10,9},{13,14},{14,13},{17,18},{18,... | collective-permute-start | bytes 737288 | tf_op jit(solution)/shard_map/ppermute | solution.py:42
  14.3 22.0 %collective-permute-start = (bf16[576,768]{1,0:T(8,128)(2,1)S(1)}, bf16[576,768]{1,0:T(8,128)(2,1)}, u32[]{:S(2)}, u32[]{:S(2)}) collective-permute-start(bf16[576,768]{1,0:T(8,128)(2,1)S(1)} %bitcast.14), channel_id=1, source_target_pairs={{0,4},{4,0},{8,12},{12,8},{1,5},{5,1},{9,13},{13,9},{2,6},{6,2},{1... | collective-permute-start | bytes 2654216 | tf_op jit(solution)/shard_map/ppermute | solution.py:48
  18.5 14.2 %collective-permute-start.10 = (bf16[192,768]{1,0:T(8,128)(2,1)}, bf16[192,768]{1,0:T(8,128)(2,1)S(1)}, u32[]{:S(2)}, u32[]{:S(2)}) collective-permute-start(bf16[192,768]{1,0:T(8,128)(2,1)} %copy-done.3), channel_id=1, source_target_pairs={{0,8},{4,12},{8,0},{12,4},{1,9},{5,13},{9,1},{13,5},{2,10},{6,14},... | collective-permute-start | bytes 884744 | tf_op jit(solution)/shard_map/ppermute | solution.py:48
  19.6 13.2 %collective-permute-start.8 = (bf16[192,768]{1,0:T(8,128)(2,1)}, bf16[192,768]{1,0:T(8,128)(2,1)S(1)}, u32[]{:S(2)}, u32[]{:S(2)}) collective-permute-start(bf16[192,768]{1,0:T(8,128)(2,1)} %collective-permute-done.1.refs_2_), channel_id=1, source_target_pairs={{0,16},{16,0},{1,17},{17,1},{2,18},{18,2},{3,19},{19,3},{4,20},{20... | collective-permute-start | bytes 884744 | tf_op jit(solution)/shard_map/ppermute | solution.py:519
  21.2 6.1 %collective-permute-start.6 = (bf16[8,768]{1,0:T(8,128)(2,1)S(1)}, bf16[8,768]{1,0:T(8,128)(2,1)S(1)}, u32[]{:S(2)}, u32[]{:S(2)}) collective-permute-start(bf16[8,768]{1,0:T(8,128)(2,1)S(1)} %pad_maximum_fusion.1), channel_id=1, source_target_pairs={{0,2},{1,3},{2,0},{3,1},{4,6},{5,7},{6,4},{7,5},{8,10},{9,11},{10,... | collective-permute-start | bytes 36872 | tf_op jit(solution)/shard_map/ppermute | solution.py:48
  27.3 5.9 %copy-start.4 = (bf16[768,192]{0,1:T(8,128)(2,1)S(1)}, bf16[768,192]{0,1:T(8,128)(2,1)}, u32[]{:S(2)}) copy-start(bf16[768,192]{0,1:T(8,128)(2,1)} %param.8) | copy-start | bytes 884740
  29.9 6.2 %collective-permute-start.7 = (bf16[192,768]{1,0:T(8,128)(2,1)}, bf16[192,768]{1,0:T(8,128)(2,1)S(1)}, u32[]{:S(2)}, u32[]{:S(2)}) collective-permute-start(bf16[192,768]{1,0:T(8,128)(2,1)} %collective-permute-done.1.refs_2_), channel_id=1, source_target_pairs={{0,4},{4,0},{8,12},{12,8},{1,5},{5,1},{9,13},{13,9},{2,6},{6,2},{1... | collective-permute-start | bytes 884744 | tf_op jit(solution)/shard_map/ppermute | solution.py:48
  32.7 3.6 %collective-permute-start.11 = (bf16[192,768]{1,0:T(8,128)(2,1)S(1)}, bf16[192,768]{1,0:T(8,128)(2,1)S(1)}, u32[]{:S(2)}, u32[]{:S(2)}) collective-permute-start(bf16[192,768]{1,0:T(8,128)(2,1)S(1)} %collective-permute-done.10.refs_6_), channel_id=1, source_target_pairs={{0,4},{4,0},{8,12},{12,8},{1,5},{5,1},{9,13},{13,9},{2,6},{6,2},{1... | collective-permute-start | bytes 884744 | tf_op jit(solution)/shard_map/ppermute | solution.py:48
  32.7 3.6 %collective-permute-start.9 = (bf16[192,768]{1,0:T(8,128)(2,1)S(1)}, bf16[192,768]{1,0:T(8,128)(2,1)S(1)}, u32[]{:S(2)}, u32[]{:S(2)}) collective-permute-start(bf16[192,768]{1,0:T(8,128)(2,1)S(1)} %collective-permute-done.8.refs_4_), channel_id=1, source_target_pairs={{0,4},{4,0},{8,12},{12,8},{1,5},{5,1},{9,13},{13,9},{2,6},{6,2},{1... | collective-permute-start | bytes 884744 | tf_op jit(solution)/shard_map/ppermute | solution.py:48
  33.2 12.0 %collective-permute-start.13 = (bf16[208,768]{1,0:T(8,128)(2,1)S(1)}, bf16[208,768]{1,0:T(8,128)(2,1)S(1)}, u32[]{:S(2)}, u32[]{:S(2)}) collective-permute-start(bf16[208,768]{1,0:T(8,128)(2,1)S(1)} %pad_maximum_fusion.refs_0_), channel_id=1, source_target_pairs={{0,8},{4,12},{8,0},{12,4},{1,9},{5,13},{9,1},{13,5},{2,10},{6,14},... | collective-permute-start | bytes 958472 | tf_op jit(solution)/shard_map/ppermute | solution.py:48
  36.1 9.5 %collective-permute-start.12 = (bf16[208,768]{1,0:T(8,128)(2,1)S(1)}, bf16[208,768]{1,0:T(8,128)(2,1)S(1)}, u32[]{:S(2)}, u32[]{:S(2)}) collective-permute-start(bf16[208,768]{1,0:T(8,128)(2,1)S(1)} %pad_maximum_fusion.refs_0_), channel_id=1, source_target_pairs={{0,4},{4,0},{8,12},{12,8},{1,5},{5,1},{9,13},{13,9},{2,6},{6,2},{1... | collective-permute-start | bytes 958472 | tf_op jit(solution)/shard_map/ppermute | solution.py:48
  45.2 1.7 %collective-permute-start.14 = (bf16[208,768]{1,0:T(8,128)(2,1)S(1)}, bf16[208,768]{1,0:T(8,128)(2,1)S(1)}, u32[]{:S(2)}, u32[]{:S(2)}) collective-permute-start(bf16[208,768]{1,0:T(8,128)(2,1)S(1)} %collective-permute-done.13.refs_2_), channel_id=1, source_target_pairs={{0,4},{4,0},{8,12},{12,8},{1,5},{5,1},{9,13},{13,9},{2,6},{6,2},{1... | collective-permute-start | bytes 958472 | tf_op jit(solution)/shard_map/ppermute | solution.py:48
